TPU v7x, 128 devices: a whole 4x4x4 slice. The times are simulated.
128 devices in a mesh: ctx: 16 (over x_hi, y, core), shard: 8 (over z, x_lo).
Axes of the slice: x: 4 (x_hi: 2, x_lo: 2; x = x_hi * 2 + x_lo), y: 4, z: 4, core: 2. Of those that a mesh axis runs over, the one named last changes fastest.
Arguments:
- inputs: bfloat16 [8, 2048, 768], P('shard', 'ctx'), may hold values from -6 to 6
- cotangent: bfloat16 [8, 2048, 768], P('shard', 'ctx'), may hold values from -6 to 6
- attention_in: float32 [768, 2304], P('shard'), may hold values from -0.21875 to 0.21875
- attention_out: float32 [768, 768], P('shard'), may hold values from -1.25 to 1.25
- expand_weight: float32 [768, 3072], P('shard'), may hold values from -0.21875 to 0.21875
- contract_weight: float32 [3072, 768], P('shard'), may hold values from -0.109375 to 0.109375
- vectors: float32 [12, 768], P(None, 'shard'), may hold values from -0.8 to 1.5, as said below
- first_attention_in: float32 [768, 2304], P('shard'), may hold values from -48 to 48
- first_attention_out: float32 [768, 768], P('shard'), may hold values from -8 to 8
- first_expand_weight: float32 [768, 3072], P('shard'), may hold values from -24 to 24
- first_contract_weight: float32 [3072, 768], P('shard'), may hold values from -56 to 56
- first_vectors: float32 [12, 768], P(None, 'shard'), may hold values from -64 to 64
- second_attention_in: float32 [768, 2304], P('shard'), may hold values from 311.296 to 1245.184
- second_attention_out: float32 [768, 768], P('shard'), may hold values from 9.28 to 36.8
- second_expand_weight: float32 [768, 3072], P('shard'), may hold values from 77.0048 to 311.296
- second_contract_weight: float32 [3072, 768], P('shard'), may hold values from 360.448 to 1458.176
- second_vectors: float32 [12, 768], P(None, 'shard'), may hold values from 425.984 to 1638.4
Outputs:
- layer_output: bfloat16 [8, 2048, 768], P('shard', 'ctx')
- input_grad: float32 [8, 2048, 768], P('shard', 'ctx')
- new_first_attention_in: float32 [768, 2304], P('shard')
- new_second_attention_in: float32 [768, 2304], P('shard')
- new_attention_in: float32 [768, 2304], P('shard')
- new_first_attention_out: float32 [768, 768], P('shard')
- new_second_attention_out: float32 [768, 768], P('shard')
- new_attention_out: float32 [768, 768], P('shard')
- new_first_expand_weight: float32 [768, 3072], P('shard')
- new_second_expand_weight: float32 [768, 3072], P('shard')
- new_expand_weight: float32 [768, 3072], P('shard')
- new_first_contract_weight: float32 [3072, 768], P('shard')
- new_second_contract_weight: float32 [3072, 768], P('shard')
- new_contract_weight: float32 [3072, 768], P('shard')
- new_first_vectors: float32 [12, 768], P(None, 'shard')
- new_second_vectors: float32 [12, 768], P(None, 'shard')
- new_vectors: float32 [12, 768], P(None, 'shard')
Inputs may be any that keep to these rules, and one draw needn't show every extreme that they name: `vectors`: rows 0 and 5 (the norms' gains) lie between 0.5 and 1.5; the other rows lie between -0.8 and 0.8.
All inputs are finite; a program needn't handle non-finite values.
Results may differ from a plain program's by a relative error of at most 0.033.
Values may be sent and summed in bfloat16 or wider, within the bound.
A program may use at most 192 MiB of HBM per device.

v0:
```python
from functools import partial

import jax
import jax.numpy as jnp
from jax import lax
from jax.sharding import PartitionSpec as P

HEAD = 64
STEP = 10


norm_eps = 1e-05
beta_first = 0.9
beta_second = 0.95
adam_eps = 1e-08
decay_matrix = 0.1
rate_matrix = 0.1
rate_vector = 0.5


def gather_turned(arrays, axis, dims):
    turned = [jnp.moveaxis(a, dim, 0) for a, dim in zip(arrays, dims)]
    widths = [t[0].size for t in turned]
    both = jnp.concatenate([t.reshape(-1, w) for t, w in zip(turned, widths)], axis=1)
    out = lax.all_gather(both, axis, axis=0, tiled=True)
    blocks = jnp.split(out, [sum(widths[:k]) for k in range(1, len(widths))], axis=1)
    return tuple(
        (
            jnp.moveaxis(b.reshape(-1, *t.shape[1:]), 0, dim)
            for b, t, dim in zip(blocks, turned, dims)
        )
    )


def sent_together(arrays, axis, dim, along):
    both = jnp.concatenate(arrays, axis=along)
    out, at, gathered = (lax.all_gather(both, axis, axis=dim, tiled=True), 0, [])
    for a in arrays:
        gathered.append(lax.slice_in_dim(out, at, at + a.shape[along], axis=along))
        at += a.shape[along]
    return tuple(gathered)


def side_by_side(arrays, axis, dim, along):
    both = jnp.concatenate(arrays, axis=along)
    out, at, gathered = (lax.psum_scatter(both, axis, scatter_dimension=dim, tiled=True), 0, [])
    for a in arrays:
        gathered.append(lax.slice_in_dim(out, at, at + a.shape[along], axis=along))
        at += a.shape[along]
    return tuple(gathered)


def layer_norm(values, scale_row, shift_row):
    average = jnp.mean(values, -1, keepdims=True)
    centred = values - average
    variance = jnp.mean(centred * centred, -1, keepdims=True)
    return centred * lax.rsqrt(variance + norm_eps) * scale_row + shift_row


def unpack(vector_rows):
    return [vector_rows[position] for position in range(8)] + [vector_rows[8:].reshape(-1)]


def product_over_rows(left, right):
    return lax.dot_general(
        left, right, (((0,), (0,)), ((), ())), preferred_element_type=jnp.float32
    )


def product_over_columns(left, right):
    return lax.dot_general(
        left, right, (((1,), (1,)), ((), ())), preferred_element_type=jnp.float32
    )


def adam_step(weight, moment_one, moment_two, gradient, learn_rate, decay_share):
    first_new = beta_first * moment_one + (1.0 - beta_first) * gradient
    second_new = beta_second * moment_two + (1.0 - beta_second) * gradient * gradient
    first_hat = first_new / (1.0 - beta_first**STEP)
    second_hat = second_new / (1.0 - beta_second**STEP)
    weight_new = weight - learn_rate * (
        first_hat / (jnp.sqrt(second_hat) + adam_eps) + decay_share * weight
    )
    return (first_new, second_new, weight_new)


def skip_block(state_in):
    return state_in


def on_device(
    inputs,
    cotangent,
    attention_in,
    attention_out,
    expand_weight,
    contract_weight,
    vectors,
    first_attention_in,
    first_attention_out,
    first_expand_weight,
    first_contract_weight,
    first_vectors,
    second_attention_in,
    second_attention_out,
    second_expand_weight,
    second_contract_weight,
    second_vectors,
):
    row_count = inputs.shape[1]
    model_width = inputs.shape[2]
    head_count = model_width // HEAD
    score_scale = HEAD ** (-0.5)
    seq_length = lax.axis_size("ctx") * row_count
    query_place = lax.axis_index("ctx") * row_count + jnp.arange(row_count, dtype=jnp.int32)
    tokens = inputs[0].astype(jnp.float32)
    in_full, out_full, vector_full = gather_turned(
        (
            attention_in.astype(jnp.bfloat16),
            attention_out.astype(jnp.bfloat16),
            vectors.astype(jnp.bfloat16),
        ),
        "shard",
        (0, 0, 1),
    )
    (
        gain_one,
        shift_one,
        bias_query,
        bias_value,
        bias_out,
        gain_two,
        shift_two,
        bias_down,
        bias_up,
    ) = unpack(vector_full.astype(jnp.float32))
    normed = layer_norm(tokens, gain_one, shift_one)
    normed_low = normed.astype(jnp.bfloat16)
    projected = jnp.dot(normed_low, in_full, preferred_element_type=jnp.float32)
    query_rows = (projected[:, :model_width] + bias_query).astype(jnp.bfloat16)
    key_rows = projected[:, model_width : 2 * model_width].astype(jnp.bfloat16)
    value_rows = (projected[:, 2 * model_width :] + bias_value).astype(jnp.bfloat16)
    query_heads = query_rows.reshape(row_count, head_count, HEAD)
    start_state = (
        jnp.full((head_count, row_count), -1e30, jnp.float32),
        jnp.zeros((head_count, row_count), jnp.float32),
        jnp.zeros((head_count, row_count, HEAD), jnp.float32),
    )
    key_block, value_block = sent_together((key_rows, value_rows), "ctx", 0, 1)
    block_rows = key_block.shape[0]

    def forward_visit_block(state_in):
        running_max, weight_sum, accumulated = state_in
        scores = (
            jnp.einsum(
                "qhd,khd->hqk",
                query_heads,
                key_block.reshape(block_rows, head_count, HEAD),
                preferred_element_type=jnp.float32,
            )
            * score_scale
        )
        allowed = jnp.arange(block_rows, dtype=jnp.int32)[None, :] <= query_place[:, None]
        scores = jnp.where(allowed[None], scores, -1e30)
        new_max = jnp.maximum(running_max, jnp.max(scores, -1))
        exp_scores = jnp.where(allowed[None], jnp.exp(scores - new_max[:, :, None]), 0.0)
        weight_sum = jnp.sum(exp_scores, -1)
        accumulated = jnp.einsum(
            "hqk,khd->hqd",
            exp_scores.astype(jnp.bfloat16),
            value_block.reshape(block_rows, head_count, HEAD),
            preferred_element_type=jnp.float32,
        )
        return (new_max, weight_sum, accumulated)

    running_max, weight_sum, accumulated = lax.cond(
        jnp.int32(0) <= query_place[-1], forward_visit_block, skip_block, start_state
    )
    log_total = running_max + jnp.log(weight_sum)
    attended = (
        (accumulated / weight_sum[:, :, None]).transpose(1, 0, 2).reshape(row_count, model_width)
    )
    attended_low = attended.astype(jnp.bfloat16)
    middle = tokens + jnp.dot(attended_low, out_full, preferred_element_type=jnp.float32) + bias_out
    expand_full, contract_full = (
        lax.all_gather(expand_weight.astype(jnp.bfloat16), "shard", axis=0, tiled=True),
        lax.all_gather(contract_weight.astype(jnp.bfloat16), "shard", axis=0, tiled=True),
    )
    normed_two = layer_norm(middle, gain_two, shift_two)
    normed_two_low = normed_two.astype(jnp.bfloat16)
    hidden_pre = jnp.dot(normed_two_low, expand_full, preferred_element_type=jnp.float32) + bias_up
    active_low = jax.nn.gelu(hidden_pre, approximate=True).astype(jnp.bfloat16)
    result = (
        middle + jnp.dot(active_low, contract_full, preferred_element_type=jnp.float32) + bias_down
    )
    expand_back, contract_back = (expand_full, contract_full)
    grad_result_low = cotangent[0]
    grad_result = grad_result_low.astype(jnp.float32)
    grad_contract = product_over_rows(active_low, grad_result_low)
    grad_bias_down = jnp.sum(grad_result, 0)
    grad_active = product_over_columns(grad_result_low, contract_back)
    grad_pre = jax.vjp(partial(jax.nn.gelu, approximate=True), hidden_pre)[1](grad_active)[0]
    grad_pre_low = grad_pre.astype(jnp.bfloat16)
    grad_bias_up = jnp.sum(grad_pre_low, 0, dtype=jnp.float32)
    grad_expand = product_over_rows(normed_two_low, grad_pre_low)
    grad_normed_two = product_over_columns(grad_pre_low, expand_back)
    grad_middle_norm, grad_gain_two, grad_shift_two = jax.vjp(
        layer_norm, middle, gain_two, shift_two
    )[1](grad_normed_two)
    grad_middle = grad_result + grad_middle_norm
    in_back, out_back = (in_full, out_full)
    grad_branch_low = grad_middle.astype(jnp.bfloat16)
    grad_bias_out = jnp.sum(grad_branch_low, 0, dtype=jnp.float32)
    grad_attention_out = product_over_rows(attended_low, grad_branch_low)
    grad_attended_low = product_over_columns(grad_branch_low, out_back).astype(jnp.bfloat16)
    grad_out_heads = grad_attended_low.reshape(row_count, head_count, HEAD)
    row_delta = jnp.sum(
        (grad_attended_low.astype(jnp.float32) * attended).reshape(row_count, head_count, HEAD), -1
    ).T
    back_state = (
        jnp.zeros((row_count, head_count, HEAD), jnp.float32),
        jnp.zeros((seq_length, 2 * model_width), jnp.float32),
    )
    backward_key_block, backward_value_block = sent_together((key_rows, value_rows), "ctx", 0, 1)
    backward_block_rows = backward_key_block.shape[0]
    key_heads = backward_key_block.reshape(backward_block_rows, head_count, HEAD)
    value_heads = backward_value_block.reshape(backward_block_rows, head_count, HEAD)

    def backward_visit_block(state_in):
        scores = (
            jnp.einsum("qhd,khd->hqk", query_heads, key_heads, preferred_element_type=jnp.float32)
            * score_scale
        )
        allowed = jnp.arange(backward_block_rows, dtype=jnp.int32)[None, :] <= query_place[:, None]
        probabilities = jnp.where(allowed[None], jnp.exp(scores - log_total[:, :, None]), 0.0)
        grad_values = jnp.einsum(
            "hqk,qhd->khd",
            probabilities.astype(jnp.bfloat16),
            grad_out_heads,
            preferred_element_type=jnp.float32,
        )
        grad_probs = jnp.einsum(
            "qhd,khd->hqk", grad_out_heads, value_heads, preferred_element_type=jnp.float32
        )
        grad_scores = (probabilities * (grad_probs - row_delta[:, :, None])).astype(jnp.bfloat16)
        grad_query = (
            jnp.einsum("hqk,khd->qhd", grad_scores, key_heads, preferred_element_type=jnp.float32)
            * score_scale
        )
        grad_keys = (
            jnp.einsum("hqk,qhd->khd", grad_scores, query_heads, preferred_element_type=jnp.float32)
            * score_scale
        )
        update = jnp.concatenate(
            [
                grad_keys.reshape(backward_block_rows, model_width),
                grad_values.reshape(backward_block_rows, model_width),
            ],
            1,
        )
        return (grad_query, update)

    grad_query, grad_pairs = lax.cond(
        jnp.int32(0) <= query_place[-1], backward_visit_block, skip_block, back_state
    )
    own_pairs = lax.psum_scatter(
        grad_pairs.astype(jnp.bfloat16), "ctx", scatter_dimension=0, tiled=True
    )
    grad_query_low = grad_query.reshape(row_count, model_width).astype(jnp.bfloat16)
    grad_mixed_low = jnp.concatenate([grad_query_low, own_pairs], 1)
    grad_bias_query = jnp.sum(grad_query_low, 0, dtype=jnp.float32)
    grad_bias_value = jnp.sum(own_pairs[:, model_width:], 0, dtype=jnp.float32)
    grad_attention_in = product_over_rows(normed_low, grad_mixed_low)
    grad_normed = product_over_columns(grad_mixed_low, in_back)
    grad_tokens_norm, grad_gain_one, grad_shift_one = jax.vjp(
        layer_norm, tokens, gain_one, shift_one
    )[1](grad_normed)
    input_grad = grad_middle + grad_tokens_norm
    grad_vectors = jnp.concatenate(
        [
            jnp.stack(
                [
                    grad_gain_one,
                    grad_shift_one,
                    grad_bias_query,
                    grad_bias_value,
                    grad_bias_out,
                    grad_gain_two,
                    grad_shift_two,
                    grad_bias_down,
                ]
            ),
            grad_bias_up.reshape(-1, model_width),
        ],
        0,
    )
    every_part = (
        *tuple(
            (
                part.astype(jnp.float32)
                for part in side_by_side(
                    (
                        grad_attention_in.astype(jnp.bfloat16),
                        grad_attention_out.astype(jnp.bfloat16),
                    ),
                    "shard",
                    0,
                    1,
                )
            )
        ),
        lax.psum_scatter(
            grad_vectors.astype(jnp.bfloat16), "shard", scatter_dimension=1, tiled=True
        ).astype(jnp.float32),
        lax.psum_scatter(
            grad_expand.astype(jnp.bfloat16), "shard", scatter_dimension=0, tiled=True
        ).astype(jnp.float32),
        lax.psum_scatter(
            grad_contract.astype(jnp.bfloat16), "shard", scatter_dimension=0, tiled=True
        ).astype(jnp.float32),
    )
    shard_in, shard_out, shard_vectors, shard_expand, shard_contract = (
        lax.psum(every_part[0].astype(jnp.bfloat16), "ctx").astype(jnp.float32),
        lax.psum(every_part[1].astype(jnp.bfloat16), "ctx").astype(jnp.float32),
        lax.psum(every_part[2].astype(jnp.bfloat16), "ctx").astype(jnp.float32),
        lax.psum(every_part[3].astype(jnp.bfloat16), "ctx").astype(jnp.float32),
        lax.psum(every_part[4].astype(jnp.bfloat16), "ctx").astype(jnp.float32),
    )
    new_in = adam_step(
        attention_in, first_attention_in, second_attention_in, shard_in, rate_matrix, decay_matrix
    )
    new_out = adam_step(
        attention_out,
        first_attention_out,
        second_attention_out,
        shard_out,
        rate_matrix,
        decay_matrix,
    )
    new_expand = adam_step(
        expand_weight,
        first_expand_weight,
        second_expand_weight,
        shard_expand,
        rate_matrix,
        decay_matrix,
    )
    new_contract = adam_step(
        contract_weight,
        first_contract_weight,
        second_contract_weight,
        shard_contract,
        rate_matrix,
        decay_matrix,
    )
    new_table = adam_step(vectors, first_vectors, second_vectors, shard_vectors, rate_vector, 0.0)
    return (
        result.astype(jnp.bfloat16)[None],
        input_grad[None],
        new_in[0],
        new_in[1],
        new_in[2],
        new_out[0],
        new_out[1],
        new_out[2],
        new_expand[0],
        new_expand[1],
        new_expand[2],
        new_contract[0],
        new_contract[1],
        new_contract[2],
        new_table[0],
        new_table[1],
        new_table[2],
    )


def solution(mesh):
    in_specs = (
        P("shard", "ctx", None),
        P("shard", "ctx", None),
        P("shard", None),
        P("shard", None),
        P("shard", None),
        P("shard", None),
        P(None, "shard"),
        P("shard", None),
        P("shard", None),
        P("shard", None),
        P("shard", None),
        P(None, "shard"),
        P("shard", None),
        P("shard", None),
        P("shard", None),
        P("shard", None),
        P(None, "shard"),
    )
    out_specs = (
        P("shard", "ctx", None),
        P("shard", "ctx", None),
        P("shard", None),
        P("shard", None),
        P("shard", None),
        P("shard", None),
        P("shard", None),
        P("shard", None),
        P("shard", None),
        P("shard", None),
        P("shard", None),
        P("shard", None),
        P("shard", None),
        P("shard", None),
        P(None, "shard"),
        P(None, "shard"),
        P(None, "shard"),
    )
    return jax.shard_map(
        on_device, mesh=mesh, in_specs=in_specs, out_specs=out_specs, check_vma=False
    )
```

profile of v0, /device:TPU:1, one launch (start us, length us, event | category | flops | bytes accessed | tf_op | source)
XLA Modules:
  0.0 1063.6 jit_solution(8498965668229682383)
XLA Ops:
  8.1 1.0 convert_element_type.146
  9.1 1.2 convert_element_type.145
  12.1 106.5 %all-gather.5.cloned.1.call-done = bf16[768,3084]{1,0:T(8,128)(2,1)} async-done(((bf16[96,3084]{1,0:T(8,128)(2,1)}), bf16[768,3084]{1,0:T(8,128)(2,1)}) %all-gather.5.cloned.1.call-update) | async-done | bytes 4737040 | tf_op jit(solution)/shard_map/all_gather | solution.py:25
  118.6 1.0 convert_bitcast_fusion.1
  119.5 1.6 slice_reduce_fusion.2
  121.7 2.8 fusion.21
  129.8 60.5 %all-gather.7.cloned.1.call-done = bf16[2048,1536]{1,0:T(8,128)(2,1)} async-done(((bf16[128,1536]{1,0:T(8,128)(2,1)}), bf16[2048,1536]{1,0:T(8,128)(2,1)}) %all-gather.7.cloned.1.call-update) | async-done | bytes 6291472 | tf_op jit(solution)/shard_map/all_gather | solution.py:37
  190.3 5.0 fusion.89
  195.3 33.0 %conditional.2 = (f32[12,128]{1,0:T(8,128)}, f32[12,128]{1,0:T(8,128)}, f32[12,128,64]{1,2,0:T(8,128)S(1)}, f32[12,128]{1,0:T(8,128)S(1)}) conditional(s32[]{:T(128)} %bitcast.12, () %tuple.26, (s32[128]{0:T(128)}, bf16[2048,768]{1,0:T(8,128)(2,1)}, bf16[128,12,64]{0,2,1:T(8,128)(2,1)S(1)}, bf16[2048,768]{1,0:T(8,128)(2,1)S(1)}) %tuple.102), branch_computations={%region_2.0_spmd, %region_3.6_spmd} | conditional | flops 846461440 | bytes 71944816 | solution.py:176
  195.3 3.0 copy.58
  198.2 0.9 iota_compare_fusion
  199.2 4.7 copy.57
  203.8 8.9 fusion
  213.3 6.5 fusion.3
  219.8 7.5 fusion.2
  229.1 1.0 broadcast_divide_fusion
  230.1 0.9 copy.60
  231.0 1.9 fusion.90
  234.2 56.2 %all-gather.9.cloned.1.call-done = bf16[768,3072]{1,0:T(8,128)(2,1)} async-done(((bf16[96,3072]{1,0:T(8,128)(2,1)}), bf16[768,3072]{1,0:T(8,128)(2,1)}) %all-gather.9.cloned.1.call-update) | async-done | bytes 4718608 | tf_op jit(solution)/shard_map/all_gather | solution.py:186
  290.3 4.3 convolution_add_fusion
  294.7 98.4 %all-gather.11.cloned.1.call-done = bf16[3072,768]{1,0:T(8,128)(2,1)} async-done(((bf16[384,768]{1,0:T(8,128)(2,1)}), bf16[3072,768]{1,0:T(8,128)(2,1)}) %all-gather.11.cloned.1.call-update) | async-done | bytes 4718608 | tf_op jit(solution)/shard_map/all_gather | solution.py:187
  393.0 5.6 fusion.91
  398.7 2.3 multiply_reduce_fusion
  403.3 2.6 convert_multiply_fusion.3
  406.0 1.9 copy.61
  407.9 1.6 reduce_sum.177
  409.5 38.0 %conditional.3 = (bf16[2048,1536]{0,1:T(8,128)(2,1)}, bf16[128,768]{0,1:T(8,128)(2,1)}, bf16[1,768]{1,0:T(2,128)(2,1)}) conditional(s32[]{:T(128)} %bitcast.12, () %tuple.28, (s32[128]{0:T(128)}, bf16[2048,768]{1,0:T(8,128)(2,1)}, bf16[128,12,64]{0,2,1:T(8,128)(2,1)}, f32[12,128]{1,0:T(8,128)}, f32[12,128]{1,0:T(8,128)}, ...), branch_computations={%region_11.12_spmd, %region_12.13_spmd} | conditional | flops 2061009664 | bytes 127558848 | solution.py:263
  409.5 1.3 add.161
  410.8 1.7 copy.63
  412.5 1.5 iota_compare_fusion.1
  414.1 3.0 copy.64
  417.1 3.2 copy.62
  420.3 2.8 fusion.92
  423.1 8.3 multiply_convert_fusion
  431.4 4.6 fusion.10
  436.1 3.5 bitcast_reduce_fusion
  439.6 1.0 convolution_multiply_fusion
  440.6 1.3 stack.29
  441.9 5.5 pad_maximum_fusion
  447.5 8.6 copy.67
  456.2 0.9 copy-done.6
  457.6 87.3 %reduce-scatter.16.cloned.1.call-done = bf16[128,1536]{1,0:T(8,128)(2,1)} async-done(((bf16[2048,1536]{1,0:T(8,128)(2,1)}), bf16[128,1536]{1,0:T(8,128)(2,1)}) %reduce-scatter.16.cloned.1.call-update) | async-done | bytes 393232
  544.9 1.2 copy.68
  546.1 2.2 convolution_convert_fusion.2
  548.3 2.8 pad_maximum_fusion.1
  551.4 1.2 copy-done.2
  552.5 3.8 convolution_convert_fusion
  556.4 1.1 copy-done.18
  557.5 4.3 convolution_convert_fusion.1
  562.6 3.5 fusion.75
  568.2 84.1 %reduce-scatter.10.cloned.1.call-done = bf16[96,3072]{1,0:T(8,128)(2,1)} async-done(((bf16[768,3072]{1,0:T(8,128)(2,1)}), bf16[96,3072]{1,0:T(8,128)(2,1)}) %reduce-scatter.10.cloned.1.call-update) | async-done | bytes 589840 | tf_op jit(solution)/shard_map/reduce_scatter | solution.py:46
  652.3 1.6 slice.91
  653.9 1.8 slice.90
  655.7 100.3 %reduce-scatter.14.cloned.1.call-done = bf16[384,768]{1,0:T(8,128)(2,1)} async-done(((bf16[3072,768]{1,0:T(8,128)(2,1)}), bf16[384,768]{1,0:T(8,128)(2,1)}) %reduce-scatter.14.cloned.1.call-update) | async-done | bytes 589840 | tf_op jit(solution)/shard_map/reduce_scatter | solution.py:318
  756.0 103.7 %reduce-scatter.12.cloned.1.call-done = bf16[96,3072]{1,0:T(8,128)(2,1)} async-done(((bf16[768,3072]{1,0:T(8,128)(2,1)}), bf16[96,3072]{1,0:T(8,128)(2,1)}) %reduce-scatter.12.cloned.1.call-update) | async-done | bytes 589840 | tf_op jit(solution)/shard_map/reduce_scatter | solution.py:315
  859.8 4.1 fusion.37
  864.0 1.0 add_bitcast_fusion
  864.9 29.9 %reduce-scatter.18.cloned.1.call-done = bf16[96,12]{1,0:T(8,128)(2,1)} async-done(((bf16[768,12]{1,0:T(8,128)(2,1)}), bf16[96,12]{1,0:T(8,128)(2,1)}) %reduce-scatter.18.cloned.1.call-update) | async-done | bytes 2320
  895.6 38.8 %psum.39 = bf16[12,96]{1,0:T(8,128)(2,1)S(1)} all-reduce(bf16[12,96]{1,0:T(8,128)(2,1)S(1)} %copy.70), channel_id=1, replica_groups=mesh['ctx'=16,'shard'=8] {'ctx'}, use_global_device_ids=true, to_apply=%region_33.34 | all-reduce | flops 1152 | bytes 4608 | tf_op jit(solution)/shard_map/psum | solution.py:325
  935.1 109.9 %all-reduce.3.cloned.1.call-done = (bf16[96,2304]{1,0:T(8,128)(2,1)}, bf16[96,768]{1,0:T(8,128)(2,1)}, bf16[96,3072]{1,0:T(8,128)(2,1)}, bf16[384,768]{1,0:T(8,128)(2,1)}) async-done(((bf16[96,2304]{1,0:T(8,128)(2,1)}, bf16[96,768]{1,0:T(8,128)(2,1)}, bf16[96,3072]{1,0:T(8,128)(2,1)}, bf16[384,768]{1,0:T(8,128)(2,1)}), (bf16[96,2304]{1,0:T(8,128)(2,1)}, bf16[96,768]{1,0:T(8,128)(2,1)}, ...) | async-done | bytes 1769488 | tf_op jit(solution)/shard_map/psum | solution.py:323
  1045.0 2.1 multiply_subtract_fusion.3
  1047.1 3.6 multiply_subtract_fusion.2
  1050.8 2.4 multiply_subtract_fusion.1
  1054.2 2.4 multiply_subtract_fusion
  (190 shorter events, 19.5 us)
Async XLA Ops:
  7.2 4.1 copy-start.3
  7.2 111.4 %all-gather.5.cloned.1.call-start = ((), (), s32[]{:S(2)}) async-start(), calls=%async_computation.5 | async-start | bytes 5529600 | tf_op jit(solution)/shard_map/all_gather | solution.py:25
  11.2 179.1 %all-gather.7.cloned.1.call-start = ((), (), s32[]{:S(2)}) async-start(), calls=%async_computation.6 | async-start | bytes 6684672 | tf_op jit(solution)/shard_map/all_gather | solution.py:37
  11.4 113.1 %copy-start.41 = (f32[128]{0:T(128)}, f32[128]{0:T(128)S(1)}, u32[]{:S(2)}) copy-start(f32[128]{0:T(128)S(1)} %broadcast_multiply_fusion.1) | copy-start | bytes 1540
  12.1 112.5 %copy-start.52 = (f32[128]{0:T(128)}, f32[128]{0:T(128)S(1)}, u32[]{:S(2)}) copy-start(f32[128]{0:T(128)S(1)} %fusion.68) | copy-start | bytes 1540
  121.7 3.8 copy-start.7
  124.5 1.9 copy-start.9
  125.4 164.9 %all-gather.9.cloned.1.call-start = ((), (), s32[]{:S(2)}) async-start(), calls=%async_computation.7 | async-start | bytes 5308416 | tf_op jit(solution)/shard_map/all_gather | solution.py:186
  126.4 266.6 %all-gather.11.cloned.1.call-start = ((), (), s32[]{:S(2)}) async-start(), calls=%async_computation.8 | async-start | bytes 5308416 | tf_op jit(solution)/shard_map/all_gather | solution.py:187
  127.4 417.5 %reduce-scatter.16.cloned.1.call-start = ((), (), s32[]{:S(2)}) async-start(), calls=%async_computation.12 | async-start | bytes 6684672
  127.4 2.4 copy-start.56
  129.8 65.5 %copy-start.11 = (bf16[128,768]{0,1:T(8,128)(2,1)}, bf16[128,768]{0,1:T(8,128)(2,1)S(1)}, u32[]{:S(2)}) copy-start(bf16[128,768]{0,1:T(8,128)(2,1)S(1)} %copy.56) | copy-start | bytes 589828
  195.3 3.0 copy-start.57
  203.8 9.5 copy-start.16
  203.8 9.5 copy-start.21
  230.1 0.9 copy-start.5
  393.0 5.6 copy-start.1
  393.0 5.6 copy-start.40
  398.6 2.3 copy-start.17
  398.6 2.3 copy-start.63
  398.6 3.3 copy-start.19
  398.7 4.7 copy-start.24
  401.2 0.8 copy-start.13
  401.2 1.4 copy-start.58
  420.3 2.9 copy-start.34
  420.3 2.9 copy-start.35
  420.3 2.9 copy-start.47
  420.3 2.9 copy-start.48
  431.4 4.6 copy-start
  436.1 3.5 copy-start.12
  456.1 1.0 copy-start.6
  456.1 1.0 copy-start.23
  456.1 90.0 %copy-start.4 = (bf16[1,128,768]{2,1,0:T(8,128)(2,1)S(1)}, bf16[1,128,768]{2,1,0:T(8,128)(2,1)}, u32[]{:S(2)}) copy-start(bf16[1,128,768]{2,1,0:T(8,128)(2,1)} %param.21) | copy-start | bytes 589828
  456.1 90.0 %copy-start.39 = (f32[768]{0:T(1024)S(1)}, f32[768]{0:T(1024)}, u32[]{:S(2)}) copy-start(f32[768]{0:T(1024)} %copy-done.38) | copy-start | bytes 9220
  456.1 90.0 %copy-start.42 = (f32[128]{0:T(128)S(1)}, f32[128]{0:T(128)}, u32[]{:S(2)}) copy-start(f32[128]{0:T(128)} %copy-done.41) | copy-start | bytes 1540
  456.1 90.0 %copy-start.53 = (f32[128]{0:T(128)S(1)}, f32[128]{0:T(128)}, u32[]{:S(2)}) copy-start(f32[128]{0:T(128)} %copy-done.52) | copy-start | bytes 1540
  456.1 196.1 %reduce-scatter.10.cloned.1.call-start = ((), (), s32[]{:S(2)}) async-start(), calls=%async_computation.9 | async-start | bytes 5308416 | tf_op jit(solution)/shard_map/reduce_scatter | solution.py:46
  551.1 1.4 copy-start.2
  551.1 1.4 copy-start.20
  551.1 204.8 %reduce-scatter.14.cloned.1.call-start = ((), (), s32[]{:S(2)}) async-start(), calls=%async_computation.11 | async-start | bytes 5308416 | tf_op jit(solution)/shard_map/reduce_scatter | solution.py:318
  556.3 1.1 copy-start.18
  556.4 303.3 %reduce-scatter.12.cloned.1.call-start = ((), (), s32[]{:S(2)}) async-start(), calls=%async_computation.10 | async-start | bytes 5308416 | tf_op jit(solution)/shard_map/reduce_scatter | solution.py:315
  561.8 0.8 copy-start.43
  561.8 333.0 %reduce-scatter.18.cloned.1.call-start = ((), (), s32[]{:S(2)}) async-start(), calls=%async_computation.13 | async-start | bytes 221184
  562.5 3.7 copy-start.61
  562.6 3.7 copy-start.54
  566.1 293.7 %copy-start.55 = (f32[768]{0:T(1024)S(1)}, f32[768]{0:T(1024)}, u32[]{:S(2)}) copy-start(f32[768]{0:T(1024)} %get-tuple-element.117) | copy-start | bytes 9220
  568.2 476.8 %all-reduce.3.cloned.1.call-start = ((), (), s32[]{:S(2)}) async-start(), calls=%async_computation.14 | async-start | bytes 3538944 | tf_op jit(solution)/shard_map/psum | solution.py:323
  859.7 4.2 copy-start.14
  859.7 4.2 copy-start.59
  859.8 74.7 %copy-start.37 = (f32[12,96]{1,0:T(8,128)S(1)}, f32[12,96]{1,0:T(8,128)}, u32[]{:S(2)}) copy-start(f32[12,96]{1,0:T(8,128)} %param.27) | copy-start | bytes 13828
  859.8 74.7 %copy-start.49 = (f32[12,96]{1,0:T(8,128)S(1)}, f32[12,96]{1,0:T(8,128)}, u32[]{:S(2)}) copy-start(f32[12,96]{1,0:T(8,128)} %param.37) | copy-start | bytes 13828
  859.8 74.7 %copy-start.50 = (f32[12,96]{1,0:T(8,128)S(1)}, f32[12,96]{1,0:T(8,128)}, u32[]{:S(2)}) copy-start(f32[12,96]{1,0:T(8,128)} %param.32) | copy-start | bytes 13828
  859.8 185.2 %copy-start.26 = (f32[96,768]{1,0:T(8,128)S(1)}, f32[96,768]{1,0:T(8,128)}, u32[]{:S(2)}) copy-start(f32[96,768]{1,0:T(8,128)} %param.24) | copy-start | bytes 884740
  859.8 185.2 %copy-start.33 = (f32[96,768]{1,0:T(8,128)S(1)}, f32[96,768]{1,0:T(8,128)}, u32[]{:S(2)}) copy-start(f32[96,768]{1,0:T(8,128)} %param.34) | copy-start | bytes 884740
  863.9 183.2 %copy-start.15 = (f32[96,2304]{1,0:T(8,128)S(1)}, f32[96,2304]{1,0:T(8,128)}, u32[]{:S(2)}) copy-start(f32[96,2304]{1,0:T(8,128)} %param.23) | copy-start | bytes 2654212
  1047.1 3.7 copy-start.8
  1047.1 3.7 copy-start.27
  1047.1 3.7 copy-start.28
  1047.1 3.7 copy-start.32
  1050.8 2.5 copy-start.10
  1050.8 2.5 copy-start.29
  1050.8 3.2 copy-start.30
  1050.8 3.4 copy-start.31
  (10 other events, 6.6 us)
Sparse Core Ops, SparseCore 0:
  11.3 107.1 all-gather.4
  125.6 64.6 all-gather.6
  192.5 97.7 all-gather.8
  292.4 100.5 all-gather.10
  456.3 88.5 reduce-scatter.15
  551.3 100.9 reduce-scatter.9
  654.8 101.0 reduce-scatter.13
  758.5 101.1 reduce-scatter.11
  862.7 32.0 reduce-scatter.17
  898.0 146.9 all-reduce.2
where the time goes:
time: 1070 us; the launch traced here: 1060 us
  waiting for transfers between devices  837 us (78%)
  matrix products  73.4 us (7%)
  local copies, waits for them, and re-layouts  53.1 us (5%)
  other arithmetic  44.8 us (4%)
  blocking collectives  38.8 us (4%)
  between operations  15.7 us (1%)
    unnamed x12, waiting for transfers between devices  117 us
    psum x1, waiting for transfers between devices, on_device(): lax.psum(every_part[0].astype(jnp.bfloat16), 'ctx').astype(jnp.float32)  110 us
    all_gather x1, waiting for transfers between devices, gather_turned(): out = lax.all_gather(both, axis, axis=0, tiled=True)  106 us
    reduce_scatter x1, waiting for transfers between devices, on_device(): lax.psum_scatter(grad_expand.astype(jnp.bfloat16), 'shard', scatter_dimen...  104 us
    reduce_scatter x1, waiting for transfers between devices, on_device(): lax.psum_scatter(grad_contract.astype(jnp.bfloat16), 'shard', scatter_dim...  100 us
    all_gather x1, waiting for transfers between devices, on_device(): lax.all_gather(contract_weight.astype(jnp.bfloat16), 'shard', axis=0, til...  98.4 us
    reduce_scatter x1, waiting for transfers between devices, side_by_side(): lax.psum_scatter(both, axis, scatter_dimension=dim, tiled=True)  84.1 us
    all_gather x1, waiting for transfers between devices, sent_together(): lax.all_gather(both, axis, axis=dim, tiled=True)  60.5 us
  transfers between devices with their start and end apart: 10, of which 10 were waited for; matrix products, arithmetic and copies ran while one was open for 7% of the time, Pallas kernels for 0%

commit v1 on v0

v1 whole, which is shorter than its diff:
```python
from functools import partial

import jax
import jax.numpy as jnp
from jax import lax
from jax.experimental import pallas as pl
from jax.experimental.pallas import tpu as pltpu
from jax.sharding import PartitionSpec as P

HEAD = 64
STEP = 10
LANES = 128
GROUP_ROWS = (192, 288)
IN_AT, OUT_AT, VEC_AT = 0, 864, 1440
EXP_AT, CON_AT = 0, 1152
EARLY, OUT_EARLY, VEC_LATE = 2, 192, 672
PART_ROWS = 96
STREAMS = {192: (64, 64, 64), 288: (192, 64, 32), 96: (32, 32, 32)}
MIB = 2**20

norm_eps = 1e-05
beta_first = 0.9
beta_second = 0.95
adam_eps = 1e-08
decay_matrix = 0.1
rate_matrix = 0.1
rate_vector = 0.5

MESH = pl.DeviceIdType.MESH
BF = jnp.bfloat16
F32 = jnp.float32


class Place:
    def __init__(self):
        ctx = lax.axis_index("ctx")
        shard = lax.axis_index("shard")
        self.core = lax.rem(ctx, 2)
        xh, xl = lax.div(ctx, 8), lax.rem(shard, 2)
        self.at = (xh * 2 + xl, lax.rem(lax.div(ctx, 2), 4), lax.div(shard, 2))

    def move(self, axis, by):
        return lax.rem(self.at[axis] + by + 4, 4)

    def device(self, at, core):
        x, y, z = at
        return {
            "ctx": (lax.div(x, 2) * 4 + y) * 2 + core,
            "shard": z * 2 + lax.rem(x, 2),
        }

    def neighbour(self, axis, by):
        at = list(self.at)
        at[axis] = self.move(axis, by)
        return self.device(at, self.core)

    def along(self, axis, by):
        at = list(self.at)
        at[axis] = self.move(axis, by)
        return self.device(at, self.core)

    def of_sequence(self, by_x, by_y, other=0):
        at = (self.move(0, by_x), self.move(1, by_y), self.at[2])
        return self.device(at, 1 - self.core if other else self.core)

    def sibling(self):
        return self.device(self.at, 1 - self.core)


def greet(others):
    barrier = pltpu.get_barrier_semaphore()
    for other in others:
        pl.semaphore_signal(barrier, inc=1, device_id=other, device_id_type=MESH)


def meet(others):
    pl.semaphore_wait(pltpu.get_barrier_semaphore(), len(others))


class Links:
    def __init__(self, send, recv, used=None):
        self.send, self.recv, self.open = send, recv, []
        self.used = [0] if used is None else used

    def branch(self):
        return Links(self.send, self.recv, self.used)

    def take(self, count):
        first = self.used[0]
        self.used[0] += count
        return list(range(first, first + count))

    def copy(self, src, dst, slot, device):
        return pltpu.make_async_remote_copy(
            src_ref=src,
            dst_ref=dst,
            send_sem=self.send.at[slot],
            recv_sem=self.recv.at[slot],
            device_id=device,
            device_id_type=MESH,
        )

    def start(self, src, dst, slot, device):
        made = self.copy(src, dst, slot, device)
        made.start()
        self.open.append(made)

    def arrived(self, dst, slot, device):
        self.copy(dst, dst, slot, device).wait_recv()

    def close(self):
        for made in self.open:
            made.wait_send()
        self.open = []


def step(flows):
    for flow in list(flows):
        try:
            next(flow)
        except StopIteration:
            flows.remove(flow)


def in_step(flows):
    while flows:
        step(flows)


def ring_gather(links, place, axis, block):
    left, right = place.neighbour(axis, -1), place.neighbour(axis, 1)
    s = links.take(6)
    links.start(block(0, 0), block(0, 0), s[0], right)
    links.start(block(0, 1), block(0, 1), s[1], left)
    links.start(block(0, 1), block(0, 1), s[2], right)
    links.start(block(0, 0), block(0, 0), s[3], left)
    yield
    links.arrived(block(-1, 0), s[0], left)
    links.start(block(-1, 0), block(-1, 0), s[4], right)
    links.arrived(block(1, 1), s[1], right)
    links.start(block(1, 1), block(1, 1), s[5], left)
    yield
    links.arrived(block(-1, 1), s[2], left)
    links.arrived(block(1, 0), s[3], right)
    links.arrived(block(2, 0), s[4], left)
    links.arrived(block(2, 1), s[5], right)


def direct_gather(links, place, axis, block):
    s = links.take(3)
    for by in (2, 1, 3):
        links.start(block(0, None), block(0, None), s[by - 1], place.along(axis, by))
    yield
    for by in (1, 3, 2):
        links.arrived(block(-by, None), s[by - 1], place.along(axis, -by))


def ring_reduce(links, place, axis, block, from_left, from_right, got_left, got_right, add, finish):
    left, right = place.neighbour(axis, -1), place.neighbour(axis, 1)
    s = links.take(6)
    links.start(block(2, 0), from_right, s[0], left)
    links.start(block(2, 1), from_left, s[1], right)
    links.start(block(1, 0), got_left(0), s[2], right)
    links.start(block(-1, 1), got_right(1), s[3], left)
    yield
    links.arrived(from_right, s[0], right)
    add(from_right, block(-1, 0))
    links.start(from_right, got_right(0), s[4], left)
    links.arrived(from_left, s[1], left)
    add(from_left, block(1, 1))
    links.start(from_left, got_left(1), s[5], right)
    yield
    links.arrived(got_left(0), s[2], left)
    links.arrived(got_right(1), s[3], right)
    links.arrived(got_right(0), s[4], right)
    links.arrived(got_left(1), s[5], left)
    finish()


def far_exchange(links, place, source, target, over_left, over_right):
    left, right = place.neighbour(0, -1), place.neighbour(0, 1)
    s = links.take(4)
    links.start(source(0), over_left, s[0], right)
    links.start(source(1), over_right, s[1], left)
    yield
    links.arrived(over_left, s[0], left)
    links.start(over_left, target(1, 0), s[2], right)
    links.arrived(over_right, s[1], right)
    links.start(over_right, target(-1, 1), s[3], left)
    yield
    links.arrived(target(0, 0), s[2], left)
    links.arrived(target(0, 1), s[3], right)


def loop_over(sizes, body, index=()):
    if not sizes:
        body(index)
        return

    @pl.loop(0, sizes[0])
    def _(i):
        loop_over(sizes[1:], body, (*index, i))


def add_all(target, *terms):
    lead = target.shape[:-2]
    whole = len(lead) > 0 and lead[-1] * target.shape[-2] * target.shape[-1] <= 4 * 96 * LANES

    def body(index):
        total = terms[0][index].astype(F32)
        for term in terms[1:]:
            total = total + term[index].astype(F32)
        target[index] = total.astype(target.dtype)

    loop_over(lead[:-1] if whole else lead, body)


def add_into(target, term):
    add_all(target, target, term)


def halved(ref, half):
    if half is None:
        return ref
    size = ref.shape[0] // 2
    return ref.at[pl.ds(half * size, size)]


ORDERS = ((0, 1, 2), (1, 2, 0), (2, 0, 1))
LAYOUTS = tuple(order[::-1] for order in ORDERS)


def stream_rows(rows, stream):
    size = STREAMS[rows][stream]
    return pl.ds(sum(STREAMS[rows][:stream]), size)


def stream_buffers(rows):
    return [pltpu.VMEM((4, 4, 4, size, LANES), BF) for size in STREAMS[rows]]


def pieces(refs, stream, free, fixed, half=None):
    index = tuple(fixed[axis] for axis in LAYOUTS[stream] if axis not in free)
    return halved(refs[stream].at[index], half)


def held(ref, stream, outer, free, fixed, half=None):
    index = tuple(fixed[a] for a in LAYOUTS[stream] if a in outer and a not in free)
    return halved(ref.at[index], half)


def places(ref, lead, start, count):
    streams = isinstance(ref, (list, tuple))
    sizes = [r.shape[-2] for r in ref] if streams else [ref.shape[-2]]
    rows = sum(sizes)
    found = []
    while count:
        piece, inner = divmod(start, rows)
        stream = 0
        while inner >= sizes[stream]:
            inner -= sizes[stream]
            stream += 1
        size = min(sizes[stream] - inner, count)
        if streams:
            at = (piece // 4 * 2 + lead[1], piece % 4, lead[0])
            index, target = tuple(at[axis] for axis in LAYOUTS[stream]), ref[stream]
        else:
            index, target = (*lead, piece // 4, piece % 4), ref
        found.append((target, (*index, pl.ds(inner, size)), size))
        start, count = start + size, count - size
    return found


def load_rows(ref, lead, start, count):
    parts = [target[index] for target, index, _ in places(ref, lead, start, count)]
    return parts[0] if len(parts) == 1 else jnp.concatenate(parts, 0)


def store_rows(ref, lead, start, value):
    at = 0
    for target, index, size in places(ref, lead, start, value.shape[0]):
        target[index] = value[at : at + size]
        at += size


def half_of(core, first, second):
    return jnp.where(core == 0, first, second).astype(BF)


def pack_attention(core, inward, outward, table, own):
    for j in range(9):
        at = (j // 3) * 768 + (j % 3) * LANES
        tile = half_of(core, inward[:, at : at + LANES], inward[:, at + 384 : at + 384 + LANES])
        store_rows(own, (), IN_AT + 96 * j, tile)
    for j in range(6):
        tile = outward[:, j * LANES : (j + 1) * LANES].astype(BF)
        store_rows(own, (), OUT_AT + 96 * j, tile)
    wide = jnp.concatenate([table[...], jnp.zeros((12, LANES - 96), F32)], 1)
    store_rows(own, (), VEC_AT, jnp.concatenate([wide, jnp.zeros((4, LANES), F32)], 0).astype(BF))
    store_rows(own, (), VEC_AT + 16, jnp.zeros((80, LANES), BF))


def pack_hidden(core, expand, contract, own):
    for pair in range(4):
        at = pair * 768
        wide = [
            half_of(core, expand[:, at + k : at + k + 192], expand[:, at + k + 192 : at + k + 384])
            for k in (0, 384)
        ]
        wide = jnp.concatenate(wide, 1)
        for j in range(3):
            store_rows(own, (), EXP_AT + 96 * (3 * pair + j), wide[:, j * LANES : (j + 1) * LANES])
    for j in range(6):
        at = slice(j * LANES, (j + 1) * LANES)
        store_rows(own, (), CON_AT + 192 * j, half_of(core, contract[:192, at], contract[192:, at]))


def gather_flow(links, place, out, stream):
    for phase, axis in enumerate(ORDERS[stream]):
        free = ORDERS[stream][:phase]

        def block(offset, half, axis=axis, free=free):
            at = list(place.at)
            at[axis] = place.move(axis, offset)
            return pieces(out, stream, free, at, half)

        yield from (direct_gather if phase < 2 else ring_gather)(links, place, axis, block)


def over_ctx(links, place, first, ref_at, over_left, over_right):
    xh, y = lax.div(place.at[0], 2), place.at[1]

    def by_y(whole):
        def block(offset, half):
            return ref_at(None if whole else xh, place.move(1, offset), half)

        yield from ring_gather(links, place, 1, block)

    def by_x(whole):
        yy = None if whole else y

        def source(half):
            return ref_at(xh, yy, half)

        def target(by, half):
            return ref_at(1 - lax.div(place.move(0, by), 2), yy, half)

        yield from far_exchange(links, place, source, target, over_left, over_right)

    if first == "x":
        yield from by_x(False)
        yield from by_y(True)
    else:
        yield from by_y(False)
        yield from by_x(True)


KV_ROWS = ((0, 160), (160, 96))


def gather_pairs_flow(links, place, out, group, over_left, over_right):
    def at(xh, y, half):
        index = (y, xh) if group == 0 else (xh, y)
        return halved(out.at[tuple(i for i in index if i is not None)], half)

    yield from over_ctx(links, place, "xy"[group], at, over_left, over_right)


def reduce_pairs_flow(links, place, part, out, group, buffers):
    from_left, from_right, got_left, got_right, total, over_left, over_right, far = buffers
    begin, count = KV_ROWS[group]
    xh = lax.div(place.at[0], 2)
    target = out.at[pl.ds(begin, count)]

    def ring(block, finish):
        yield from ring_reduce(
            links, place, 1, block, from_left, from_right,
            lambda half: halved(got_left, half),
            lambda half: halved(got_right, half),
            add_into, finish,
        )

    def exchange(source):
        yield from far_exchange(
            links, place, lambda half: halved(source, half), lambda by, half: halved(far, half),
            over_left, over_right,
        )

    terms = part if group == 0 else total

    def block(offset, half):
        return halved(terms.at[place.move(1, offset)], half)

    if group == 0:
        yield from ring(block, lambda: add_all(total, block(0, None), got_left, got_right))
        yield from exchange(total.at[1 - xh])
        add_all(target, total.at[xh], far)
    else:
        yield from exchange(part.at[1 - xh])
        add_all(total, part.at[xh], far)
        yield from ring(block, lambda: add_all(target, block(0, None), got_left, got_right))


def pairs_scratch(width):
    (_, a), (_, b) = KV_ROWS

    def vmem(*shape):
        return pltpu.VMEM((*shape, width), BF)

    first = [vmem(1, a)] * 2 + [vmem(2, a)] * 3 + [vmem(a // 2)] * 2 + [vmem(a)]
    second = [vmem(b // 2)] * 2 + [vmem(b)] * 2 + [vmem(4, b)] + [vmem(2, b)] * 2 + [vmem(4, b)]
    return first, second


def sum_flow(links, place, part, out, stream, buffers, ring):
    rows = out.shape[-2]
    order = ORDERS[stream]
    term = None
    for phase, axis in enumerate(reversed(order)):
        free = order[: 2 - phase]
        outer = order[: 3 - phase]
        count = 5 if ring and phase == 0 else 4
        mine, buffers = buffers[:count], buffers[count:]
        total = mine[-1]
        if phase == 2:
            at = (place.core, lax.div(place.at[0], 2), place.at[1])
            total = out.at[(*at, stream_rows(rows, stream))]

        def block(offset, half, axis=axis, free=free, outer=outer, term=term):
            at = list(place.at)
            at[axis] = place.move(axis, offset)
            if term is None:
                return pieces(part, stream, free, at, half)
            return held(term, stream, outer, free, at, half)

        if count == 5:
            from_left, from_right, got_left, got_right = mine[:4]

            def finish(block=block, total=total, got_left=got_left, got_right=got_right):
                add_all(total, block(0, None), got_left, got_right)

            yield from ring_reduce(
                links, place, axis, block, from_left, from_right,
                lambda half, got_left=got_left: halved(got_left, half),
                lambda half, got_right=got_right: halved(got_right, half),
                add_into, finish,
            )
        else:
            s = links.take(3)
            for by in (2, 1, 3):
                links.start(block(by, None), mine[by - 1], s[by - 1], place.along(axis, by))
            yield
            for by in (1, 3, 2):
                links.arrived(mine[by - 1], s[by - 1], place.along(axis, -by))
            add_all(total, block(0, None), *mine[:3])
        term = total


def sum_scratch(rows, ring):
    scratch = []
    for size in STREAMS[rows]:
        for phase in range(3):
            lead = (4,) * (2 - phase)
            full = pltpu.VMEM((*lead, size, LANES), BF)
            if ring and phase == 0:
                scratch += [pltpu.VMEM((2, 4, size, LANES), BF)] * 2 + [full] * 3
            else:
                scratch += [full] * 4
    return scratch


def group_flow(links, place, part, out, scratch, ring, at_once):
    count = len(scratch) // 3
    flows = [
        sum_flow(links, place, part, out, s, scratch[count * s : count * (s + 1)], ring)
        for s in range(3)
    ]
    while flows:
        step(flows)
        if flows:
            yield
    yield from (spread_at_once if at_once else spread_flow)(links, place, out)


def spread_at_once(links, place, out):
    core, xh, y = place.core, lax.div(place.at[0], 2), place.at[1]
    mine = out.at[core, xh, y]
    moves = [(bx, by, other) for other in (0, 1) for bx in (0, 2) for by in range(4)][1:]
    s = links.take(15)
    for slot, (bx, by, other) in zip(s, moves):
        links.start(mine, mine, slot, place.of_sequence(bx, by, other))
    yield
    for slot, (bx, by, other) in zip(s, moves):
        theirs = out.at[
            1 - core if other else core, lax.div(place.move(0, -bx), 2), place.move(1, -by)
        ]
        links.arrived(theirs, slot, place.of_sequence(-bx, -by, other))


def spread_flow(links, place, out):
    core, xh, y = place.core, lax.div(place.at[0], 2), place.at[1]
    mine = out.at[core, xh, y]
    moves = [(bx, by) for bx in (0, 2) for by in range(4) if (bx, by) != (0, 0)]
    s = links.take(8)
    for slot, (bx, by) in zip(s, moves):
        links.start(mine, mine, slot, place.of_sequence(bx, by))
    yield
    for slot, (bx, by) in zip(s, moves):
        theirs = out.at[core, lax.div(place.move(0, -bx), 2), place.move(1, -by)]
        links.arrived(theirs, slot, place.of_sequence(-bx, -by))
    links.start(out.at[core], out.at[core], s[7], place.sibling())
    yield
    links.arrived(out.at[1 - core], s[7], place.sibling())


def nt(left, right):
    return lax.dot_general(left, right, (((1,), (1,)), ((), ())), preferred_element_type=F32)


def nn(left, right):
    return jnp.dot(left, right, preferred_element_type=F32)


def causal(core):
    key = lax.broadcasted_iota(jnp.int32, (256, 256), 0)
    query = lax.broadcasted_iota(jnp.int32, (256, 256), 1)
    shift = core * 128
    return lax.rem(key + shift, 256) <= lax.rem(query + shift, 256)


def one_head(tile, which):
    lane = lax.broadcasted_iota(jnp.int32, tile.shape, 1)
    return jnp.where((lane < HEAD) == (which == 0), tile, jnp.zeros_like(tile))


def masked_heads(q_ref, masked):
    for p in range(masked.shape[0] // 2):
        tile = q_ref[:, p * LANES : (p + 1) * LANES] * jnp.asarray(0.125, BF)
        for h in range(2):
            masked[2 * p + h] = one_head(tile, h)


def attend_blocks(p, blocks, allowed, masked, top, mass, acc):
    values = [kv[:, LANES:].T for kv in blocks]
    scores = [[nt(kv[:, :LANES], masked[2 * p + h]) for kv in blocks] for h in range(2)]
    later = []
    for h in range(2):
        head = 2 * p + h
        part = [value[h * HEAD : (h + 1) * HEAD] for value in values]
        if allowed is not None:
            score = jnp.where(allowed, scores[h][0], -1e30)
            high = jnp.max(score, 0, keepdims=True)
            weights = jnp.exp(score - high)
            top[head] = high
            mass[head] = jnp.sum(weights, 0, keepdims=True)
            acc[head] = nn(part[0], weights.astype(BF))
            continue
        old = top[head]
        new = old
        for score in scores[h]:
            new = jnp.maximum(new, jnp.max(score, 0, keepdims=True))
        fade = jnp.exp(old - new)
        top[head] = new
        total, low = mass[head] * fade, []
        for score in scores[h]:
            weight = jnp.exp(score - new)
            total = total + jnp.sum(weight, 0, keepdims=True)
            low.append(weight.astype(BF))
        mass[head] = total
        later.append((head, fade, part, low))
    for head, fade, part, low in later:
        mixed = acc[head] * fade
        for value, weight in zip(part, low):
            mixed = mixed + nn(value, weight)
        acc[head] = mixed


def earlier_blocks(chip, visit, between):
    between(0)

    @pl.loop(0, lax.div(chip, 2))
    def _(j):
        xh, y = lax.div(j, 2), 2 * lax.rem(j, 2)
        visit([(xh, y), (xh, y + 1)])

    between(1)

    @pl.loop(0, lax.rem(chip, 2))
    def _(j):
        visit([(lax.div(chip, 4), 2 * lax.div(lax.rem(chip, 4), 2))])


def read_block(pairs, p, xh, y):
    return jnp.concatenate([pairs[0][p, y, xh], pairs[1][p, xh, y]], 0)


def write_block(pairs, p, xh, y, value):
    cut = KV_ROWS[1][0]
    pairs[0][p, y, xh] = value[:cut]
    pairs[1][p, xh, y] = value[cut:]


def attend_end(p, o_ref, low_ref, top, mass, acc):
    both = jnp.concatenate([acc[2 * p + h] / mass[2 * p + h] for h in range(2)], 0)
    out = both.T
    o_ref[:, p * LANES : (p + 1) * LANES] = out
    low_ref[:, p * LANES : (p + 1) * LANES] = out.astype(BF)
    for head in (2 * p, 2 * p + 1):
        top[head] = top[head] + jnp.log(mass[head])


def attend_back(p, chip, core, pairs, o_ref, go_ref, lse, dq_ref, masked, masked_go, delta, acc, between):
    at = slice(p * LANES, (p + 1) * LANES)
    go = go_ref[:, at]
    product = (go.astype(F32) * o_ref[:, at]).T
    for h in range(2):
        head = 2 * p + h
        masked_go[head] = one_head(go, h)
        delta[head] = jnp.sum(product[h * HEAD : (h + 1) * HEAD], 0, keepdims=True)
        acc[head] = jnp.zeros(acc.shape[1:], F32)

    def visit(blocks, allowed=None):
        found = [read_block(pairs, p, xh, y) for xh, y in blocks]
        turned = [kv[:, :LANES].T for kv in found]
        scores = [[nt(kv[:, :LANES], masked[2 * p + h]) for h in range(2)] for kv in found]
        grads = [[nt(kv[:, LANES:], masked_go[2 * p + h]) for h in range(2)] for kv in found]
        low, low_grads = [], []
        for b in range(2):
            for h in range(2):
                score = scores[b][h]
                if allowed is not None:
                    score = jnp.where(allowed[b], score, -1e30)
                weights = jnp.exp(score - lse[2 * p + h])
                low_grads.append((weights * (grads[b][h] - delta[2 * p + h])).astype(BF))
                low.append(weights.astype(BF))
        for b, (xh, y) in enumerate(blocks):
            grad_keys = grad_values = None
            for h in range(2):
                head = 2 * p + h
                more_values = nn(low[2 * b + h], masked_go[head])
                more_keys = nn(low_grads[2 * b + h], masked[head])
                grad_values = more_values if h == 0 else grad_values + more_values
                grad_keys = more_keys if h == 0 else grad_keys + more_keys
            write_block(pairs, p, xh, y, jnp.concatenate([grad_keys, grad_values], 1).astype(BF))
        for h in range(2):
            head = 2 * p + h
            mixed = acc[head]
            for b in range(2):
                mixed = mixed + nn(turned[b][h * HEAD : (h + 1) * HEAD], low_grads[2 * b + h])
            acc[head] = mixed

    def two(j):
        xh, y = lax.div(j, 2), 2 * lax.rem(j, 2)
        return [(xh, y), (xh, y + 1)]

    odd = lax.rem(chip, 2) == 1
    below = causal(core)
    visit(two(lax.div(chip, 2)), [below | odd, below & odd])
    between(0)

    @pl.loop(0, lax.div(chip, 2))
    def _(j):
        visit(two(j))

    between(1)

    @pl.loop(chip + 1, 8)
    def _(j):
        write_block(
            pairs, p, lax.div(j, 4), lax.rem(j, 4), jnp.zeros((256, 2 * LANES), BF)
        )

    both = jnp.concatenate([acc[2 * p], acc[2 * p + 1]], 0) * 0.125
    dq_ref[:, at] = both.T.astype(BF)


def norm_parts(values):
    centred = values - jnp.mean(values, -1, keepdims=True)
    spread = lax.rsqrt(jnp.mean(centred * centred, -1, keepdims=True) + norm_eps)
    return centred * spread, spread


def norm_back(grad, unit, spread, gain):
    scaled = grad * gain
    return spread * (
        scaled
        - jnp.mean(scaled, -1, keepdims=True)
        - unit * jnp.mean(scaled * unit, -1, keepdims=True)
    )


def mine_of(core, row):
    return jnp.where(core == 0, row[:, :384], row[:, 384:])


def read_attention(wa, inward, outward, table):
    rows = []
    for s in range(8):
        lead = (s // 2, s % 2)
        for j in range(9):
            inward[96 * s : 96 * s + 96, j * LANES : (j + 1) * LANES] = load_rows(
                wa, lead, IN_AT + 96 * j, 96
            )
        for j in range(6):
            outward[96 * s : 96 * s + 96, j * LANES : (j + 1) * LANES] = load_rows(
                wa, lead, OUT_AT + 96 * j, 96
            )
        rows.append(load_rows(wa, lead, VEC_AT, 16).astype(F32)[:, :96])
    table[...] = jnp.concatenate(rows, 1)


def read_hidden(wb, expand, contract):
    for s in range(8):
        lead = (s // 2, s % 2)
        for j in range(12):
            expand[96 * s : 96 * s + 96, j * LANES : (j + 1) * LANES] = load_rows(
                wb, lead, EXP_AT + 96 * j, 96
            )
        for j in range(6):
            contract[192 * s : 192 * s + 192, j * LANES : (j + 1) * LANES] = load_rows(
                wb, lead, CON_AT + 192 * j, 192
            )


def project(core, own, other, inward, table, query, pairs, xh, y, normed):
    tokens = jnp.concatenate([own[0], other[0]], 0).astype(F32)
    unit, _ = norm_parts(tokens)
    low = (unit * table[0:1, :] + table[1:2, :]).astype(BF)
    normed[...] = low
    query[...] = (nn(low, inward[:, :384]) + mine_of(core, table[2:3, :])).astype(BF)
    keys = nn(low, inward[:, 384:768]).astype(BF)
    values = (nn(low, inward[:, 768:]) + mine_of(core, table[3:4, :])).astype(BF)
    for p in range(3):
        at = slice(p * LANES, (p + 1) * LANES)
        write_block(pairs, p, xh, y, jnp.concatenate([keys[:, at], values[:, at]], 1))


def bias_up_of(core, table):
    parts = []
    for s in range(8):
        row = table[8 + s // 2 : 9 + s // 2, :]
        at = 384 * (s % 2)
        parts.append(jnp.where(core == 0, row[:, at : at + 192], row[:, at + 192 : at + 384]))
    return jnp.concatenate(parts, 1)


def out_rows(outward, core):
    return outward[pl.ds(pl.multiple_of(core * 384, 128), 384), :]


def hidden_layer(
    core, own, other, cot, cot_other, attended, attended_other, outward, table, expand, contract,
    middle, result, grad_two, grad_up, turned, active_low, grad_pre_low,
):
    tokens = jnp.concatenate([own[0], other[0]], 0).astype(F32)
    mixed = nn(attended[...], out_rows(outward, core))
    mixed = mixed + nn(attended_other[...], out_rows(outward, 1 - core))
    middle[...] = tokens + mixed + table[4:5, :]
    unit, _ = norm_parts(middle[...])
    low = (unit * table[5:6, :] + table[6:7, :]).astype(BF)
    turned[...] = low.T
    cotangent = jnp.concatenate([cot[0], cot_other[0]], 0)
    bias = bias_up_of(core, table)
    for ch in range(4):
        at = slice(384 * ch, 384 * ch + 384)
        u = nn(low, expand[:, at]) + bias[:, at]
        square = u * u
        bend = jnp.tanh(0.7978845608028654 * u * (1.0 + 0.044715 * square))
        half_up = 0.5 * (1.0 + bend)
        active = (u * half_up).astype(BF)
        slope = half_up + 0.5 * u * (1.0 - bend * bend) * (
            0.7978845608028654 * (1.0 + 0.134145 * square)
        )
        low_result = nn(active, contract[at, :])
        grad_pre = (nt(cotangent, contract[at, :]) * slope).astype(BF)
        low_two = nt(grad_pre, expand[:, at])
        active_low[:, at] = active
        grad_pre_low[:, at] = grad_pre
        if ch == 0:
            result[...] = low_result
            grad_two[...] = low_two
        else:
            result[...] = result[...] + low_result
            grad_two[...] = grad_two[...] + low_two
        grad_up[0:1, at] = jnp.sum(grad_pre.astype(F32), 0, keepdims=True)


def hidden_gradients(cot, cot_other, turned, active_low, grad_pre_low, part):
    cotangent = jnp.concatenate([cot[0], cot_other[0]], 0)
    for ch in range(4):
        at = slice(384 * ch, 384 * ch + 384)
        grad_contract = nn(active_low[:, at].T, cotangent).astype(BF)
        for k in range(2):
            for j in range(6):
                store_rows(
                    part,
                    (ch, k),
                    CON_AT + 192 * j,
                    grad_contract[192 * k : 192 * k + 192, j * LANES : (j + 1) * LANES],
                )
        grad_expand = nn(turned[...], grad_pre_low[:, at]).astype(BF)
        for s in range(8):
            for j in range(3):
                store_rows(
                    part,
                    (s // 2, s % 2),
                    EXP_AT + 96 * (3 * ch + j),
                    grad_expand[96 * s : 96 * s + 96, j * LANES : (j + 1) * LANES],
                )


def branch_back(
    core, cot, cot_other, middle, grad_two, grad_two_other, outward, table,
    grad_middle, grad_attended, grad_branch, rows,
):
    unit, spread = norm_parts(middle[...])
    mine = grad_two[...]
    cotangent = jnp.concatenate([cot[0], cot_other[0]], 0).astype(F32)
    total = cotangent + norm_back(mine + grad_two_other[...], unit, spread, table[5:6, :])
    grad_middle[...] = total
    low = total.astype(BF)
    grad_attended[...] = nt(low, out_rows(outward, core)).astype(BF)
    grad_branch[...] = low
    rows[0:1, :] = jnp.sum(low[:128].astype(F32), 0, keepdims=True)
    rows[1:2, :] = jnp.sum(mine * unit, 0, keepdims=True)
    rows[2:3, :] = jnp.sum(mine, 0, keepdims=True)
    rows[3:4, :] = jnp.sum(cotangent[:128], 0, keepdims=True)


def beside(core, row):
    blank = jnp.zeros_like(row)
    return jnp.where(
        core == 0, jnp.concatenate([row, blank], 1), jnp.concatenate([blank, row], 1)
    )


def store_inward(early, late, index, tile):
    for s in range(8):
        rows = tile[96 * s : 96 * s + 96]
        if index < EARLY:
            store_rows(early, (s // 2, s % 2), 96 * index, rows)
        else:
            store_rows(late, (s // 2, s % 2), 96 * (index - EARLY), rows)


def query_back(
    core, normed, grad_query, inward, attended, grad_branch, turned, early, late, grad_one
):
    turned[...] = normed[...].T
    grad_out = nn(attended[...].T, grad_branch[...]).astype(BF)
    grad = nn(turned[...], grad_query[...]).astype(BF)
    for j in range(3):
        store_inward(early, late, j, grad[:, j * LANES : (j + 1) * LANES])
    none = jnp.zeros((96, LANES), BF)
    for k in range(4):
        for j in range(6):
            store_rows(
                early,
                (2 * core + k // 2, k % 2),
                OUT_EARLY + 96 * j,
                grad_out[96 * k : 96 * k + 96, j * LANES : (j + 1) * LANES],
            )
            store_rows(early, (2 * (1 - core) + k // 2, k % 2), OUT_EARLY + 96 * j, none)
    grad_one[...] = nt(grad_query[...], inward[:, :384])


def pair_back(p, grad_pairs, inward, turned, early, late, grad_one):
    for k in range(2):
        grad = grad_pairs[p, :, k * LANES : (k + 1) * LANES]
        at = 384 + 384 * k + LANES * p
        store_inward(early, late, 3 * k + 3 + p, nn(turned[...], grad).astype(BF))
        grad_one[...] = grad_one[...] + nt(grad, inward[:, at : at + LANES])


def fixed_rows(core, grad_query, rows, grad_up, out):
    out[2:3, :] = beside(core, jnp.sum(grad_query[...].astype(F32), 0, keepdims=True))
    out[4:8, :] = rows[0:4, :]
    ups = [beside(core, grad_up[0:1, 192 * s : 192 * s + 192]) for s in range(8)]
    up = jnp.concatenate(ups, 1)
    for k in range(4):
        out[8 + k : 9 + k, :] = up[:, 768 * k : 768 * k + 768]
    out[12:16, :] = jnp.zeros((4, 768), F32)


def vectors_back(core, own, other, grad_pairs, grad_one, table, late):
    one = grad_one[...]
    tokens = jnp.concatenate([own[0], other[0]], 0).astype(F32)
    unit, _ = norm_parts(tokens)
    values = jnp.concatenate([grad_pairs[p, :, LANES:] for p in range(3)], 1)
    table[0:1, :] = jnp.sum(one * unit, 0, keepdims=True)
    table[1:2, :] = jnp.sum(one, 0, keepdims=True)
    table[3:4, :] = beside(core, jnp.sum(values.astype(F32), 0, keepdims=True))
    side = jnp.zeros((16, LANES - 96), F32)
    for s in range(8):
        tile = jnp.concatenate([table[:, 96 * s : 96 * s + 96], side], 1).astype(BF)
        store_rows(late, (s // 2, s % 2), VEC_LATE, tile)


def blank_rows(late):
    for s in range(8):
        store_rows(late, (s // 2, s % 2), VEC_LATE + 16, jnp.zeros((80, LANES), BF))


def adam_step(weight, moment_one, moment_two, gradient, learn_rate, decay_share):
    first_new = beta_first * moment_one + (1.0 - beta_first) * gradient
    second_new = beta_second * moment_two + (1.0 - beta_second) * gradient * gradient
    first_hat = first_new / (1.0 - beta_first**STEP)
    second_hat = second_new / (1.0 - beta_second**STEP)
    weight_new = weight - learn_rate * (
        first_hat / (jnp.sqrt(second_hat) + adam_eps) + decay_share * weight
    )
    return (first_new, second_new, weight_new)


def update(arrays, index, gradient):
    weight, first, second = arrays
    first[index], second[index], weight[index] = adam_step(
        weight[index], first[index], second[index], gradient.astype(F32), rate_matrix, decay_matrix
    )


def update_inward(early, late, inward, index):
    got, start = (early, 96 * index) if index < EARLY else (late, 96 * (index - EARLY))
    for core in range(2):
        k = index // 3 * 6 + core * 3 + index % 3
        tile = load_rows(got, (core,), start, 96)
        update(inward, (slice(None), slice(k * LANES, (k + 1) * LANES)), tile)


def update_outward(got, outward):
    for j in range(6):
        both = [load_rows(got, (c,), OUT_EARLY + 96 * j, 96).astype(F32) for c in range(2)]
        update(outward, (slice(None), slice(j * LANES, (j + 1) * LANES)), both[0] + both[1])


def update_vectors(got, olds, news):
    both = [load_rows(got, (c,), VEC_LATE, 16).astype(F32) for c in range(2)]
    gradient = (both[0] + both[1])[:12, :96]
    weight, first, second = [old[...] for old in olds]
    new = adam_step(weight, first, second, gradient, rate_vector, 0.0)
    for ref, value in zip((news[1], news[2], news[0]), new):
        ref[...] = value


def update_expand(got, expand, pair):
    wide = [
        jnp.concatenate(
            [load_rows(got, (c,), EXP_AT + 96 * (3 * pair + j), 96) for j in range(3)], 1
        )
        for c in range(2)
    ]
    for k in range(2):
        at = 768 * pair + 384 * k
        tile = jnp.concatenate([w[:, 192 * k : 192 * k + 192] for w in wide], 1)
        update(expand, (slice(None), slice(at, at + 384)), tile)


def update_contract(got, contract, quarter):
    c, h = quarter // 2, quarter % 2
    for j in range(6):
        tile = load_rows(got, (c,), CON_AT + 192 * j + 96 * h, 96)
        rows = slice(96 * quarter, 96 * quarter + 96)
        update(contract, (rows, slice(j * LANES, (j + 1) * LANES)), tile)


class Named:
    def __init__(self, names, refs):
        at = 0
        for name, count in names:
            setattr(self, name, refs[at] if count is None else refs[at : at + count])
            at += 1 if count is None else count


def layer_scratch():
    a, b = GROUP_ROWS
    rows, model, half, hidden, heads = 256, 768, 384, 1536, 6
    named = {
        "inward_f32": pltpu.VMEM((96, 2304), F32),
        "outward_f32": pltpu.VMEM((96, 768), F32),
        "expand_f32": pltpu.VMEM((96, 3072), F32),
        "contract_f32": pltpu.VMEM((384, 768), F32),
        "own_a": pltpu.VMEM((2, 4, a, LANES), BF),
        "own_b": pltpu.VMEM((2, 4, b, LANES), BF),
        "wa": stream_buffers(a),
        "wb": stream_buffers(b),
        "other": pltpu.VMEM((1, 128, model), BF),
        "cot_other": pltpu.VMEM((1, 128, model), BF),
        "inward": pltpu.VMEM((model, 3 * half), BF),
        "outward": pltpu.VMEM((model, model), BF),
        "expand": pltpu.VMEM((model, hidden), BF),
        "contract": pltpu.VMEM((hidden, model), BF),
        "table": pltpu.VMEM((16, model), F32),
        "query": pltpu.VMEM((rows, half), BF),
        "normed": pltpu.VMEM((rows, model), BF),
        "pairs": [
            pltpu.VMEM((3, 4, 2, KV_ROWS[0][1], 2 * LANES), BF),
            pltpu.VMEM((3, 2, 4, KV_ROWS[1][1], 2 * LANES), BF),
        ],
        "pass_x": [pltpu.VMEM((KV_ROWS[0][1] // 2, 2 * LANES), BF)] * 6,
        "pass_y": [pltpu.VMEM((2, KV_ROWS[1][1], 2 * LANES), BF)] * 6,
        "masked": pltpu.VMEM((heads, rows, LANES), BF),
        "masked_go": pltpu.VMEM((heads, rows, LANES), BF),
        "top": pltpu.VMEM((heads, 1, rows), F32),
        "mass": pltpu.VMEM((heads, 1, rows), F32),
        "acc": pltpu.VMEM((heads, HEAD, rows), F32),
        "attended": pltpu.VMEM((rows, half), F32),
        "attended_low": pltpu.VMEM((rows, half), BF),
        "attended_other": pltpu.VMEM((rows, half), BF),
        "middle": pltpu.VMEM((rows, model), F32),
        "result": pltpu.VMEM((rows, model), F32),
        "result_other": pltpu.VMEM((128, model), F32),
        "grad_two": pltpu.VMEM((rows, model), F32),
        "grad_two_other": pltpu.VMEM((rows, model), F32),
        "grad_up": pltpu.VMEM((8, hidden), F32),
        "grad_middle": pltpu.VMEM((rows, model), F32),
        "grad_attended": pltpu.VMEM((rows, half), BF),
        "grad_branch": pltpu.VMEM((rows, model), BF),
        "grad_rows": pltpu.VMEM((8, model), F32),
        "grad_table": pltpu.VMEM((16, model), F32),
        "grad_query": pltpu.VMEM((rows, half), BF),
        "grad_pairs": pltpu.VMEM((3, rows, 2 * LANES), BF),
        "grad_one": pltpu.VMEM((rows, model), F32),
        "grad_one_other": pltpu.VMEM((128, model), F32),
        "pairs_a": pairs_scratch(2 * LANES)[0] * 3,
        "pairs_b": pairs_scratch(2 * LANES)[1] * 3,
        "turned": pltpu.VMEM((model, rows), BF),
        "active_low": pltpu.VMEM((rows, hidden), BF),
        "grad_pre_low": pltpu.VMEM((rows, hidden), BF),
        "early": stream_buffers(PART_ROWS),
        "late": stream_buffers(PART_ROWS),
        "flow_early": sum_scratch(PART_ROWS, True),
        "flow_late": sum_scratch(PART_ROWS, False),
        "flow_b": sum_scratch(b, True),
        "send": pltpu.SemaphoreType.DMA((SLOTS,)),
        "recv": pltpu.SemaphoreType.DMA((SLOTS,)),
        "local": pltpu.SemaphoreType.DMA((10,)),
    }
    names, shapes = [], []
    for name, value in named.items():
        several = isinstance(value, list)
        names.append((name, len(value) if several else None))
        shapes += value if several else [value]
    return names, shapes


SLOTS = 6 * 12 + 3 * 20 + 3 * 20 + 2 * (3 * 12 + 8) + 27 + 15 + 10


def layer_kernel(
    tokens, cot, inward, outward, expand, contract, table,
    layer, input_grad, got_b, got_early, got_late, *scratch,
):
    m = Named(layer_scratch()[0], scratch)
    place = Place()
    core, sibling = place.core, place.sibling()
    xh, y = lax.div(place.at[0], 2), place.at[1]
    chip = xh * 4 + y

    others = [place.along(axis, by) for axis in range(3) for by in (1, 2, 3)]
    others += [place.of_sequence(2, by) for by in (1, 2, 3)]
    others += [place.of_sequence(bx, by, 1) for bx in (0, 2) for by in range(4)]
    greet(others)
    loads = [
        pltpu.make_async_copy(src, dst, m.local.at[n])
        for n, (src, dst) in enumerate(
            (
                (inward, m.inward_f32),
                (outward, m.outward_f32),
                (expand, m.expand_f32),
                (contract, m.contract_f32),
            )
        )
    ]
    for load in loads:
        load.start()

    def lay_out(own, out, slot):
        copies = [
            pltpu.make_async_copy(
                own.at[xh, y, stream_rows(own.shape[-2], s)],
                pieces(out, s, (), place.at),
                m.local.at[slot + s],
            )
            for s in range(3)
        ]
        for copy in copies:
            copy.start()
        for copy in copies:
            copy.wait()

    links = Links(m.send, m.recv)

    def send_over(links, *moves):
        slots = links.take(len(moves))
        for (src, dst), slot in zip(moves, slots):
            links.start(src, dst, slot, sibling)
        return [(dst, slot) for (_, dst), slot in zip(moves, slots)]

    def wait_over(links, waits):
        for dst, slot in waits:
            links.arrived(dst, slot, sibling)

    def changed_over(src, dst):
        low, high = pl.ds(0, 128), pl.ds(128, 128)
        return (src.at[low], dst.at[high]), (src.at[high], dst.at[low])

    loads[0].wait()
    loads[1].wait()
    pack_attention(core, m.inward_f32, m.outward_f32, table, m.own_a)
    lay_out(m.own_a, m.wa, 4)
    meet(others)

    gather_a, gather_b = links.branch(), links.branch()
    flows_a = [gather_flow(gather_a, place, m.wa, s) for s in range(3)]
    flows_b = [gather_flow(gather_b, place, m.wb, s) for s in range(3)]
    step(flows_a)
    waits = send_over(links, (tokens, m.other), (cot, m.cot_other))
    loads[2].wait()
    loads[3].wait()
    pack_hidden(core, m.expand_f32, m.contract_f32, m.own_b)
    lay_out(m.own_b, m.wb, 7)
    for _ in range(2):
        step(flows_b)
        step(flows_a)
    in_step(flows_a)
    step(flows_b)
    read_attention(m.wa, m.inward, m.outward, m.table)
    wait_over(links, waits)
    project(
        core, tokens, m.other, m.inward, m.table, m.query, m.pairs, xh, y, m.normed
    )
    gather_kv = links.branch()
    kv = [
        [
            gather_pairs_flow(
                gather_kv, place, m.pairs[group].at[p], group,
                *(m.pass_x, m.pass_y)[group][2 * p : 2 * p + 2],
            )
            for group in range(2)
        ]
        for p in range(3)
    ]
    step(kv[0])
    masked_heads(m.query, m.masked)
    state = (m.masked, m.top, m.mass, m.acc)
    allowed = causal(core)
    for p in range(3):
        attend_blocks(p, [read_block(m.pairs, p, xh, y)], allowed, *state)
        for q in range(p + 1):
            step(kv[q])
        if p < 2:
            step(kv[p + 1])
    in_step(kv[0])
    step(flows_b)
    for p in range(3):

        def visit(blocks, p=p):
            attend_blocks(p, [read_block(m.pairs, p, bx, by) for bx, by in blocks], None, *state)

        def steps(k, p=p):
            for q in range(p + 1, 3):
                step(kv[q])

        earlier_blocks(chip, visit, steps)
        attend_end(p, m.attended, m.attended_low, m.top, m.mass, m.acc)
        if p < 2:
            in_step(kv[p + 1])
    waits = send_over(links, *changed_over(m.attended_low, m.attended_other))
    in_step(flows_b)
    read_hidden(m.wb, m.expand, m.contract)
    gather_a.close()
    gather_b.close()
    gather_kv.close()
    wait_over(links, waits)
    hidden_layer(
        core, tokens, m.other, cot, m.cot_other, m.attended_low, m.attended_other, m.outward,
        m.table, m.expand, m.contract, m.middle, m.result, m.grad_two, m.grad_up, m.turned,
        m.active_low, m.grad_pre_low,
    )

    waits = send_over(links, *changed_over(m.grad_two, m.grad_two_other))
    hidden_gradients(cot, m.cot_other, m.turned, m.active_low, m.grad_pre_low, m.wb)
    reduce_b, reduce_kv = links.branch(), links.branch()
    reduce_early, reduce_late = links.branch(), links.branch()

    flows_b = [group_flow(reduce_b, place, m.wb, got_b, m.flow_b, True, False)]
    step(flows_b)
    result_waits = send_over(links, (m.result.at[pl.ds(128, 128)], m.result_other))
    wait_over(links, waits)
    branch_back(
        core, cot, m.cot_other, m.middle, m.grad_two, m.grad_two_other, m.outward, m.table,
        m.grad_middle, m.grad_attended, m.grad_branch, m.grad_rows,
    )
    reduce_pairs = [
        [
            reduce_pairs_flow(
                reduce_kv, place, m.pairs[group].at[p], m.grad_pairs.at[p], group,
                (m.pairs_a, m.pairs_b)[group][8 * p : 8 * p + 8],
            )
            for group in range(2)
        ]
        for p in range(3)
    ]
    for p in range(3):

        def steps(k, p=p):
            for q in range(p):
                step(reduce_pairs[q])
            if (p, k) == (1, 0):
                step(flows_b)

        attend_back(
            p, chip, core, m.pairs, m.attended, m.grad_attended, m.top, m.grad_query,
            m.masked, m.masked_go, m.mass, m.acc, steps,
        )
        step(reduce_pairs[p])
    for flows in reduce_pairs:
        step(flows)
    query_back(
        core, m.normed, m.grad_query, m.inward, m.attended_low, m.grad_branch, m.turned, m.early,
        m.late, m.grad_one,
    )
    flows_early = [group_flow(reduce_early, place, m.early, got_early, m.flow_early, True, False)]
    step(flows_early)
    wait_over(links, result_waits)
    layer[0] = (
        m.middle[0:128, :] + (m.result[0:128, :] + m.result_other[...]) + m.table[7:8, :]
    ).astype(BF)
    fixed_rows(core, m.grad_query, m.grad_rows, m.grad_up, m.grad_table)
    blank_rows(m.late)
    for p in range(3):
        while reduce_pairs[p]:
            for flows in reduce_pairs[p:]:
                step(flows)
            if p == 2:
                step(flows_b)
            step(flows_early)
        pair_back(p, m.grad_pairs, m.inward, m.turned, m.early, m.late, m.grad_one)
    vectors_back(core, tokens, m.other, m.grad_pairs, m.grad_one, m.grad_table, m.late)
    flows_late = [group_flow(reduce_late, place, m.late, got_late, m.flow_late, False, True)]
    step(flows_late)
    waits = send_over(links, (m.grad_one.at[pl.ds(128, 128)], m.grad_one_other))
    for _ in range(2):
        step(flows_b)
        step(flows_early)
        step(flows_late)
    wait_over(links, waits)
    unit, spread = norm_parts(tokens[0].astype(F32))
    grad = m.grad_one[0:128, :] + m.grad_one_other[...]
    input_grad[0] = m.grad_middle[0:128, :] + norm_back(grad, unit, spread, m.table[0:1, :])
    while flows_b or flows_early or flows_late:
        step(flows_b)
        step(flows_early)
        step(flows_late)
    for each in (links, reduce_b, reduce_kv, reduce_early, reduce_late):
        each.close()


def update_kernel(layer_in, grad_in, got_b, got_early, got_late, *refs):
    olds = [[refs[k], refs[5 + k], refs[10 + k]] for k in range(5)]
    layer, input_grad = refs[15:17]
    news = [[refs[19 + 3 * k], refs[17 + 3 * k], refs[18 + 3 * k]] for k in range(5)]
    buffers = [refs[32 + 3 * k : 35 + 3 * k] for k in range(4)]
    sums_b, sums_early, sums_late, layer_held, grad_held = refs[44:49]
    sem = refs[49]
    used = []

    def copies(*moves, priority=0):
        made = []
        for src, dst in moves:
            copy = pltpu.make_async_copy(src, dst, sem.at[len(used)])
            copy.start(priority=priority)
            used.append(copy)
            made.append(copy)
        return made

    def wait(made):
        for copy in made:
            copy.wait()

    every = slice(None)
    first = copies((got_b, sums_b))
    chunks = [
        (2, (every, pl.ds(768 * k, 768)), partial(update_expand, sums_b, buffers[2], k))
        for k in range(4)
    ]
    chunks += [
        (3, (pl.ds(96 * k, 96), every), partial(update_contract, sums_b, buffers[3], k))
        for k in range(4)
    ]
    chunks.append((1, (every, every), partial(update_outward, sums_early, buffers[1])))

    def part(k):
        for index in range(3 * k, 3 * k + 3):
            update_inward(sums_early, sums_late, buffers[0], index)

    chunks += [(0, (every, pl.ds(768 * k, 768)), partial(part, k)) for k in range(3)]

    def load(chunk):
        n, at, _ = chunk
        return copies(*[(old.at[at], buffer.at[at]) for old, buffer in zip(olds[n], buffers[n])])

    ahead = 3
    loads = [load(chunk) for chunk in chunks[:ahead]]
    last = copies((got_early, sums_early), (got_late, sums_late))
    done = copies((layer_in, layer_held), (grad_in, grad_held))
    out = []
    wait(first)
    for k, (n, at, compute) in enumerate(chunks):
        wait(loads[k])
        if k == 8:
            wait(last + done)
            out += copies((layer_held, layer), (grad_held, input_grad))
            update_vectors(sums_late, olds[4], news[4])
        if k + ahead < len(chunks):
            loads.append(load(chunks[k + ahead]))
        compute()
        moves = [(buffer.at[at], new.at[at]) for buffer, new in zip(buffers[n], news[n])]
        out += copies(*moves, priority=1)
    wait(out)


def on_device(inputs, cotangent, *state):
    b = GROUP_ROWS[1]
    vmem = pl.BlockSpec(memory_space=pltpu.VMEM)
    ref = pl.BlockSpec(memory_space=pl.ANY)
    shapes = (
        jax.ShapeDtypeStruct(inputs.shape, BF),
        jax.ShapeDtypeStruct(inputs.shape, F32),
        jax.ShapeDtypeStruct((2, 2, 4, b, LANES), BF),
        jax.ShapeDtypeStruct((2, 2, 4, PART_ROWS, LANES), BF),
        jax.ShapeDtypeStruct((2, 2, 4, PART_ROWS, LANES), BF),
    )
    made = pl.pallas_call(
        layer_kernel,
        out_shape=shapes,
        in_specs=[vmem, vmem] + [ref] * 4 + [vmem],
        out_specs=tuple([vmem] * 5),
        scratch_shapes=layer_scratch()[1],
        compiler_params=pltpu.CompilerParams(
            collective_id=0, has_side_effects=True, vmem_limit_bytes=60 * MIB
        ),
        name="layer",
    )(inputs, cotangent, *state[:5])
    return pl.pallas_call(
        update_kernel,
        out_shape=(
            *shapes[:2],
            *[jax.ShapeDtypeStruct(w.shape, F32) for w in state[:5] for _ in range(3)],
        ),
        in_specs=[ref] * 5 + ([ref] * 4 + [vmem]) * 3,
        out_specs=tuple([ref] * 14 + [vmem] * 3),
        scratch_shapes=[
            *[pltpu.VMEM(w.shape, F32) for w in state[:4] for _ in range(3)],
            *[pltpu.VMEM(s.shape, BF) for s in shapes[2:]],
            *[pltpu.VMEM(s.shape, s.dtype) for s in shapes[:2]],
            pltpu.SemaphoreType.DMA((84,)),
        ],
        compiler_params=pltpu.CompilerParams(vmem_limit_bytes=60 * MIB),
        name="update",
    )(*made, *state)


def solution(mesh):
    tokens = P("shard", "ctx", None)
    matrix = P("shard", None)
    table = P(None, "shard")
    in_specs = (tokens, tokens) + (matrix, matrix, matrix, matrix, table) * 3
    out_specs = (tokens, tokens) + (matrix,) * 12 + (table,) * 3
    return jax.shard_map(
        on_device, mesh=mesh, in_specs=in_specs, out_specs=out_specs, check_vma=False
    )
```

time: 1070 us -> 184 us (0.17)
  waiting for transfers between devices: 837 us -> 0 us
  Pallas kernels: 0 us -> 183 us
  matrix products: 73.4 us -> 0 us
  local copies, waits for them, and re-layouts: 53.1 us -> 0 us
  other arithmetic: 44.8 us -> 0 us
  blocking collectives: 38.8 us -> 0 us
  between operations: 15.7 us -> 0.84 us
    all_gather x4 -> x0, waiting for transfers between devices: 321 us -> none  [the longest x1 106 us: gather_turned(): out = lax.all_gather(both, axis, axis=0, tiled=True)]
    reduce_scatter x3 -> x0, waiting for transfers between devices: 288 us -> none  [the longest x1 104 us: on_device(): lax.psum_scatter(grad_expand.astype(jnp.bfloat16), 'shard', scatter_dimen...]
    pallas_call x0 -> x2, Pallas kernels: none -> 183 us  [the longest x1 172 us: on_device(): pl.pallas_call(layer_kernel, out_shape=shapes, in_specs=[vmem, vmem] + [r...]
    unnamed x12 -> x0, waiting for transfers between devices: 117 us -> none
    psum x1 -> x0, waiting for transfers between devices: 110 us -> none  [on_device(): lax.psum(every_part[0].astype(jnp.bfloat16), 'ctx').astype(jnp.float32)]
    dot_general x19 -> x0, matrix products: 73.4 us -> none  [the longest x4 14 us: product_over_columns(): lax.dot_general(left, right, (((1,), (1,)), ((), ())), preferred_element_...]
    psum x1 -> x0, blocking collectives: 38.8 us -> none  [on_device(): lax.psum(every_part[2].astype(jnp.bfloat16), 'ctx').astype(jnp.float32)]
    unnamed x114 -> x0, local copies, waits for them, and re-layouts: 20 us -> none
  transfers between devices with their start and end apart: 10 -> 0, of which waited for: 10 -> 0; matrix products, arithmetic and copies ran while one was open for 7% -> 0% of each run, Pallas kernels for 0% -> 0%
where the time goes in v1:
time: 184 us
  Pallas kernels  183 us (99%)
    pallas_call x1, Pallas kernels, on_device(): pl.pallas_call(layer_kernel, out_shape=shapes, in_specs=[vmem, vmem] + [r...  172 us
    pallas_call x1, Pallas kernels, on_device(): pl.pallas_call(update_kernel, out_shape=(*shapes[:2], *[jax.ShapeDtypeStr...  11.4 us

profile of v1, /device:TPU:1, one launch (start us, length us, event | category | flops | bytes accessed | tf_op | source)
XLA Modules:
  0.0 183.8 jit_solution(6941005792621200161)
XLA Ops:
  0.7 171.6 %layer.1 = (bf16[1,128,768]{2,1,0:T(8,128)(2,1)}, f32[1,128,768]{2,1,0:T(8,128)}, bf16[2,2,4,288,128]{4,3,2,1,0:T(8,128)(2,1)}, bf16[2,2,4,96,128]{4,3,2,1,0:T(8,128)(2,1)}, bf16[2,2,4,96,128]{4,3,2,1,0:T(8,128)(2,1)}) custom-call(bf16[1,128,768]{2,1,0:T(8,128)(2,1)} %tokens.1, bf16[1,128,768]{2,1,0:T(8,128)(2,1)} %cot.1, f32[96,2304]{1,0:T(8,128)} %refs_0_.1, ...), custom_call_target="tpu_custom_call" | custom-call | tf_op jit(solution)/shard_map/layer/pallas_call | solution.py:1334
  172.3 11.4 %update.1 = (bf16[1,128,768]{2,1,0:T(8,128)(2,1)}, f32[1,128,768]{2,1,0:T(8,128)}, f32[96,2304]{1,0:T(8,128)}, f32[96,2304]{1,0:T(8,128)}, f32[96,2304]{1,0:T(8,...) custom-call(bf16[1,128,768]{2,1,0:T(8,128)(2,1)} %get-tuple-element., ...), custom_call_target="tpu_custom_call" | custom-call | tf_op jit(solution)/shard_map/update/pallas_call | solution.py:1345
